TPU v7x, 256 devices: a whole 4x4x8 slice. The times are simulated.
256 devices in a mesh: row: 8 (over z_hi, x), col: 32 (over z_lo, y, core).
Axes of the slice: x: 4, y: 4, z: 8 (z_hi: 2, z_lo: 4; z = z_hi * 4 + z_lo), core: 2. Of those that a mesh axis runs over, the one named last changes fastest.
Arguments:
- lower_panel: float32 [3, 16384, 256], P(None, ('row', 'col')), may hold values from -6 to 6
- panel_mask: int32 [3, 128], P(None, 'row'), may hold values 0 or 1
- inverse_tiles: float32 [3, 16384, 16384], P(None, 'col', 'row'), may hold values from -0.125 to 0.125
- tile_mask: int32 [3, 128, 128], P(None, 'col', 'row'), may hold values from 0 to 1, as said below
Outputs:
- inverse_panel: float32 [3, 16384, 256], P(None, ('col', 'row'))
Inputs may be any that keep to these rules, and one draw needn't show every extreme that they name: `tile_mask`: 1 marks a present block, 0 an absent one; the share of present blocks differs from block row to block row.
All inputs are finite; a program needn't handle non-finite values. No bound on the sum of `panel_mask` on one device may be relied on, other than what follows from the above.
Results may differ from a plain program's by a relative error of at most 0.00007.
Values sent between devices are 32-bit elements; how exact they have to be, the bound alone decides.
No kernel may reach another device: no remote copies, remote signals or barrier semaphores. Data moves between devices by JAX's collectives and lax.ppermute only.
A program may use at most 128 MiB of HBM per device.

v0:
```python
import jax
import jax.numpy as jnp
from jax import lax
from jax.sharding import PartitionSpec as P

highest_precision = lax.Precision.HIGHEST


def keep_rows(values, flags):
    number, total_rows, breadth = values.shape
    blocks = flags.shape[1]
    shaped = values.reshape(number, blocks, total_rows // blocks, breadth)
    return (shaped * flags.astype(jnp.float32)[:, :, None, None]).reshape(
        number, total_rows, breadth
    )


def keep_tiles(values, flags):
    number, height, breadth = values.shape
    row_blocks = flags.shape[1]
    col_blocks = flags.shape[2]
    shaped = values.reshape(
        number, row_blocks, height // row_blocks, col_blocks, breadth // col_blocks
    )
    return (shaped * flags.astype(jnp.float32)[:, :, None, :, None]).reshape(
        number, height, breadth
    )


def reduce_rows(tiles, columns):
    partial_sums = -jnp.einsum(
        "nji,niw->jnw",
        tiles,
        columns,
        precision=highest_precision,
        preferred_element_type=jnp.float32,
    )
    summed = lax.psum_scatter(partial_sums, "row", scatter_dimension=0, tiled=True)
    return jnp.transpose(summed, (1, 0, 2))


def local(lower_panel, panel_mask, inverse_tiles, tile_mask):
    number = lower_panel.shape[0]
    results = []
    for snode in range(number):
        gathered = lax.all_gather(lower_panel[snode : snode + 1], "col", axis=1, tiled=True)
        kept_panel = keep_rows(gathered, panel_mask[snode : snode + 1])
        kept_tiles = keep_tiles(inverse_tiles[snode : snode + 1], tile_mask[snode : snode + 1])
        results.append(reduce_rows(kept_tiles, kept_panel))
    return jnp.concatenate(results, axis=0)


def solution(mesh):
    return jax.shard_map(
        local,
        mesh=mesh,
        in_specs=(
            P(None, ("row", "col"), None),
            P(None, "row"),
            P(None, "col", "row"),
            P(None, "col", "row"),
        ),
        out_specs=P(None, ("col", "row"), None),
        check_vma=False,
    )
```

profile of v0, /device:TPU:6, one launch (start us, length us, event | category | flops | bytes accessed | tf_op | source)
XLA Modules:
  0.0 337.7 jit_solution(10998270870908691605)
XLA Ops:
  6.5 0.0 all-gather.4.cloned.1.call-start
  6.5 1.6 fusion.51
  8.1 0.0 all-gather.4.cloned.1.call-update
  8.1 0.0 all-gather.6.cloned.1.call-start
  8.2 0.7 all-gather.6.cloned.1.call-update
  8.9 0.0 all-gather.8.cloned.1.call-start
  8.9 0.7 all-gather.8.cloned.1.call-update
  9.6 0.0 all-reduce.6.cloned.1.call-start
  9.7 0.7 convert_bitcast_fusion.2
  10.4 2.3 mul.102
  12.7 4.9 %mul.103 = f32[1,512,2048]{2,1,0:T(8,128)} reshape(f32[4,128,16,128]{3,2,1,0:T(8,128)} %mul.102) | data formatting | bytes 8388608 | tf_op jit(solution)/shard_map/mul | solution.py:25
  17.6 2.3 mul.111
  19.9 4.9 %mul.112 = f32[1,512,2048]{2,1,0:T(8,128)} reshape(f32[4,128,16,128]{3,2,1,0:T(8,128)} %mul.111) | data formatting | bytes 8388608 | tf_op jit(solution)/shard_map/mul | solution.py:25
  24.8 2.3 mul.120
  27.1 0.0 copy-start
  27.1 4.9 %mul.121 = f32[1,512,2048]{2,1,0:T(8,128)} reshape(f32[4,128,16,128]{3,2,1,0:T(8,128)} %mul.120) | data formatting | bytes 8388608 | tf_op jit(solution)/shard_map/mul | solution.py:25
  32.0 0.0 copy-done
  32.0 0.1 broadcast_bitcast_fusion.2
  32.1 0.1 broadcast_bitcast_fusion.1
  32.2 0.1 broadcast_bitcast_fusion
  32.2 40.1 %all-gather.4.cloned.1.call-done = f32[1,2048,256]{2,1,0:T(8,128)} async-done(((f32[1,64,256]{2,1,0:T(8,128)}), f32[1,2048,256]{2,1,0:T(8,128)}) %all-gather.4.cloned.1.call-update) | async-done | bytes 2097168 | tf_op jit(solution)/shard_map/all_gather | solution.py:46
  72.4 10.8 %fusion.23 = f32[512,1,256]{0,2,1:T(8,128)S(1)} fusion(f32[1,512,2048]{2,1,0:T(8,128)} %mul.103, f32[3,512,2048]{2,1,0:T(8,128)} %param.6, f32[1,2048,256]{2,1,0:T(8,128)} %all-gather.4.cloned.1.call-done, f32[2048]{0:T(1024)S(1)} %broadcast_bitcast_fusion.2), kind=kOutput, calls=%fused_computation.19 | convolution fusion | flops 3222929408 | bytes 11018240 | tf_op jit(solution)/shard_map/nji,niw->jnw/dot_general | solution.py:31
  83.2 1.1 copy.6
  84.2 49.0 %all-gather.6.cloned.1.call-done = f32[1,2048,256]{2,1,0:T(8,128)} async-done(((f32[1,64,256]{2,1,0:T(8,128)}), f32[1,2048,256]{2,1,0:T(8,128)}) %all-gather.6.cloned.1.call-update) | async-done | bytes 2097168 | tf_op jit(solution)/shard_map/all_gather | solution.py:46
  133.3 10.8 %fusion.33 = f32[512,1,256]{0,2,1:T(8,128)S(1)} fusion(f32[1,512,2048]{2,1,0:T(8,128)} %mul.112, f32[3,512,2048]{2,1,0:T(8,128)} %param.6, f32[1,2048,256]{2,1,0:T(8,128)} %all-gather.6.cloned.1.call-done, f32[2048]{0:T(1024)S(1)} %broadcast_bitcast_fusion.1), kind=kOutput, calls=%fused_computation.21 | convolution fusion | flops 3222929408 | bytes 11018240 | tf_op jit(solution)/shard_map/nji,niw->jnw/dot_general | solution.py:31
  144.1 1.0 copy.7
  145.1 0.0 copy-start.1
  145.1 49.1 %all-gather.8.cloned.1.call-done = f32[1,2048,256]{2,1,0:T(8,128)} async-done(((f32[1,64,256]{2,1,0:T(8,128)}), f32[1,2048,256]{2,1,0:T(8,128)}) %all-gather.8.cloned.1.call-update) | async-done | bytes 2097168 | tf_op jit(solution)/shard_map/all_gather | solution.py:46
  194.2 10.8 %fusion.43 = f32[512,1,256]{0,2,1:T(8,128)S(1)} fusion(f32[1,512,2048]{2,1,0:T(8,128)} %mul.121, f32[3,512,2048]{2,1,0:T(8,128)} %param.6, f32[1,2048,256]{2,1,0:T(8,128)} %all-gather.8.cloned.1.call-done, f32[2048]{0:T(1024)S(1)} %broadcast_bitcast_fusion), kind=kOutput, calls=%fused_computation.23 | convolution fusion | flops 3222929408 | bytes 11018240 | tf_op jit(solution)/shard_map/nji,niw->jnw/dot_general | solution.py:31
  205.0 1.1 copy.8
  206.1 0.0 all-reduce.6.cloned.1.call-update
  206.1 0.0 copy-done.1
  206.1 0.6 dynamic-slice
  207.3 121.2 %all-reduce.6.cloned.1.call-done = (f32[512,1,256]{2,1,0:T(1,128)}, f32[512,1,256]{2,1,0:T(1,128)}, f32[512,1,256]{2,1,0:T(1,128)}) async-done(((f32[512,1,256]{2,1,0:T(1,128)}, f32[512,1,256]{2,1,0:T(1,128)}, f32[512,1,256]{2,1,0:T(1,128)}), (f32[512,1,256]{2,1,0:T(1,128)}, f32[512,1,256]{2,1,0:T(1,128)}, f32[512,1,256]{2,1,0:T(1,128)})) %all-reduce.6.cloned.1.call-update) | async-done | bytes 1572880
  328.5 0.8 dynamic-slice_bitcast_fusion.2
  329.3 0.9 dynamic-slice_bitcast_fusion
  330.2 0.2 pad_maximum_fusion
  330.4 0.7 copy.9
  (1 shorter events, 0.0 us)
Async XLA Ops:
  6.5 65.8 %all-gather.4.cloned.1.call-start = ((), (), s32[]{:S(2)}) async-start(), calls=%async_computation | async-start | bytes 2162688 | tf_op jit(solution)/shard_map/all_gather | solution.py:46
  8.1 125.1 %all-gather.6.cloned.1.call-start = ((), (), s32[]{:S(2)}) async-start(), calls=%async_computation.1 | async-start | bytes 2162688 | tf_op jit(solution)/shard_map/all_gather | solution.py:46
  8.9 185.3 %all-gather.8.cloned.1.call-start = ((), (), s32[]{:S(2)}) async-start(), calls=%async_computation.2 | async-start | bytes 2162688 | tf_op jit(solution)/shard_map/all_gather | solution.py:46
  9.6 318.9 %all-reduce.6.cloned.1.call-start = ((), (), s32[]{:S(2)}) async-start(), calls=%async_computation.3 | async-start | bytes 3145728
  27.1 4.9 %copy-start = (s32[3,16]{1,0:T(4,128)S(1)}, s32[3,16]{1,0:T(4,128)}, u32[]{:S(2)}) copy-start(s32[3,16]{1,0:T(4,128)} %param.5) | copy-start | bytes 580
  145.1 61.0 %copy-start.1 = (u32[256]{0:T(256)S(1)}, u32[256]{0:T(256)}, u32[]{:S(2)}) copy-start(u32[256]{0:T(256)} %constant.4) | copy-start | bytes 3076
Sparse Core Ops, SparseCore 0:
  9.2 63.1 all-gather.3
  74.2 58.9 all-gather.5
  135.1 59.0 all-gather.7
  206.2 122.2 all-reduce.5
where the time goes:
time: 338 us
  waiting for transfers between devices  261 us (77%)
  matrix products  32.4 us (10%)
  local copies, waits for them, and re-layouts  29.6 us (9%)
  between operations  13.8 us (4%)
    all_gather x3, waiting for transfers between devices, local(): lax.all_gather(lower_panel[snode:snode + 1], 'col', axis=1, tiled=True)  138 us
    unnamed x5, waiting for transfers between devices  123 us
    dot_general x3, matrix products, reduce_rows(): jnp.einsum('nji,niw->jnw', tiles, columns, precision=highest_precision, p...  32.4 us
    mul x6, local copies, waits for them, and re-layouts, keep_tiles(): shaped * flags.astype(jnp.float32)[:, :, None, :, None]  21.6 us
  transfers between devices with their start and end apart: 4, of which 4 were waited for; matrix products, arithmetic and copies ran while one was open for 14% of the time, Pallas kernels for 0%

commit v1 on v0

--- a/solution.py
+++ b/solution.py
@@ -43,7 +43,12 @@
     number = lower_panel.shape[0]
     results = []
     for snode in range(number):
-        gathered = lax.all_gather(lower_panel[snode : snode + 1], "col", axis=1, tiled=True)
+        gathered = jnp.concatenate(
+            lax.all_to_all(
+                jnp.stack([lower_panel[snode : snode + 1]] * lax.axis_size("col")), "col", 0, 0
+            ),
+            axis=1,
+        )
         kept_panel = keep_rows(gathered, panel_mask[snode : snode + 1])
         kept_tiles = keep_tiles(inverse_tiles[snode : snode + 1], tile_mask[snode : snode + 1])
         results.append(reduce_rows(kept_tiles, kept_panel))

time: 338 us -> 322 us (0.953)
  waiting for transfers between devices: 261 us -> 123 us
  blocking collectives: 0 us -> 112 us
  starting transfers between devices: 0.12 us -> 5.59 us
  matrix products: 32.4 us -> 27 us
  local copies, waits for them, and re-layouts: 29.6 us -> 34.9 us
    all_gather x3 -> x0, waiting for transfers between devices: 138 us -> none  [local(): lax.all_gather(lower_panel[snode:snode + 1], 'col', axis=1, tiled=True)]
    all_to_all x0 -> x2, blocking collectives: none -> 112 us  [local(): lax.all_to_all(jnp.stack([lower_panel[snode:snode + 1]] * lax.axis_size('...]
    all_to_all x0 -> x1, starting transfers between devices: none -> 5.55 us  [local(): lax.all_to_all(jnp.stack([lower_panel[snode:snode + 1]] * lax.axis_size('...]
    dot_general x3, matrix products: 32.4 us -> 27 us  [reduce_rows(): jnp.einsum('nji,niw->jnw', tiles, columns, precision=highest_precision, p...]
    mul x1 -> x4, other arithmetic: 0.01 us -> 4.09 us  [keep_rows(): shaped * flags.astype(jnp.float32)[:, :, None, None]]
    unnamed x5 -> x13, local copies, waits for them, and re-layouts: 0.59 us -> 4.32 us
    unnamed x5 -> x2, waiting for transfers between devices: 123 us -> 122 us
  transfers between devices with their start and end apart: 4 -> 2, of which waited for: 4 -> 2; matrix products, arithmetic and copies ran while one was open for 14% -> 15% of each run, Pallas kernels for 0% -> 0%
where the time goes in v1:
time: 322 us; the launch traced here: 321 us
  waiting for transfers between devices  123 us (38%)
  blocking collectives  112 us (35%)
  local copies, waits for them, and re-layouts  34.9 us (11%)
  matrix products  27 us (8%)
  between operations  14.2 us (4%)
  starting transfers between devices  5.59 us (2%)
  other arithmetic  4.27 us (1%)
    unnamed x2, waiting for transfers between devices  122 us
    all_to_all x2, blocking collectives, local(): lax.all_to_all(jnp.stack([lower_panel[snode:snode + 1]] * lax.axis_size('...  112 us
    dot_general x3, matrix products, reduce_rows(): jnp.einsum('nji,niw->jnw', tiles, columns, precision=highest_precision, p...  27 us
    mul x6, local copies, waits for them, and re-layouts, keep_tiles(): shaped * flags.astype(jnp.float32)[:, :, None, :, None]  21.6 us
  transfers between devices with their start and end apart: 2, of which 2 were waited for; matrix products, arithmetic and copies ran while one was open for 15% of the time, Pallas kernels for 0%

profile of v1, /device:TPU:6, one launch (start us, length us, event | category | flops | bytes accessed | tf_op | source)
XLA Modules:
  0.0 320.8 jit_solution(15949575328883180530)
XLA Ops:
  6.5 0.9 slice_bitcast_fusion.2
  7.5 0.2 stack.6
  7.7 57.6 %all_to_all.15 = f32[32,1,64,256]{3,2,1,0:T(8,128)} all-to-all(f32[32,1,64,256]{3,2,1,0:T(8,128)S(1)} %stack.6), channel_id=1, replica_groups=mesh['row'=8,'col'=32] {'col'}, dimensions={0} | all-to-all | bytes 4194304 | tf_op jit(solution)/shard_map/all_to_all | solution.py:47
  65.2 0.2 stack.7
  65.5 54.2 %all_to_all.16 = f32[32,1,64,256]{3,2,1,0:T(8,128)} all-to-all(f32[32,1,64,256]{3,2,1,0:T(8,128)S(1)} %stack.7), channel_id=1, replica_groups=mesh['row'=8,'col'=32] {'col'}, dimensions={0} | all-to-all | bytes 4194304 | tf_op jit(solution)/shard_map/all_to_all | solution.py:47
  119.7 0.0 copy-start.4
  119.7 0.0 copy-start.3
  119.7 1.6 stack.8
  121.2 5.5 %all-to-all-start.2 = ((f32[32,1,64,256]{3,2,1,0:T(8,128)}), f32[32,1,64,256]{3,2,1,0:T(8,128)S(1)}, u32[]{:S(2)}, u32[]{:S(2)}) async-start(f32[32,1,64,256]{3,2,1,0:T(8,128)} %stack.8), calls=%async_computation.2 | async-start | bytes 4194304 | tf_op jit(solution)/shard_map/all_to_all | solution.py:47
  126.8 0.0 all-reduce.6.cloned.1.call-start
  126.8 0.0 copy-done.4
  126.9 0.1 mul.109
  126.9 0.1 mul.110
  127.0 0.0 copy-done.3
  127.1 2.3 mul.115
  129.3 4.9 %mul.116 = f32[1,512,2048]{2,1,0:T(8,128)} reshape(f32[4,128,16,128]{3,2,1,0:T(8,128)} %mul.115) | data formatting | bytes 8388608 | tf_op jit(solution)/shard_map/mul | solution.py:25
  134.3 0.1 mul.119
  134.3 0.1 mul.120
  134.4 2.3 mul.125
  136.7 4.9 %mul.126 = f32[1,512,2048]{2,1,0:T(8,128)} reshape(f32[4,128,16,128]{3,2,1,0:T(8,128)} %mul.125) | data formatting | bytes 8388608 | tf_op jit(solution)/shard_map/mul | solution.py:25
  141.6 0.1 mul.129
  141.7 0.1 mul.130
  141.8 2.3 mul.135
  144.0 4.9 %mul.136 = f32[1,512,2048]{2,1,0:T(8,128)} reshape(f32[4,128,16,128]{3,2,1,0:T(8,128)} %mul.135) | data formatting | bytes 8388608 | tf_op jit(solution)/shard_map/mul | solution.py:25
  148.9 0.0 copy-start.1
  148.9 1.9 broadcast_multiply_fusion.2
  150.9 0.9 copy-done.1
  151.7 9.0 %fusion.15 = f32[512,1,256]{0,2,1:T(8,128)S(1)} fusion(f32[2048,256]{1,0:T(8,128)S(1)} %bitcast.70, f32[1,512,2048]{2,1,0:T(8,128)S(1)} %copy-done.1, f32[3,512,2048]{2,1,0:T(8,128)} %param.6), kind=kOutput, calls=%fused_computation.13 | convolution fusion | flops 3222405120 | bytes 11010048 | tf_op jit(solution)/shard_map/nji,niw->jnw/dot_general | solution.py:31
  160.7 1.1 copy.7
  161.8 0.0 copy-start.2
  161.8 1.9 broadcast_multiply_fusion.1
  163.8 0.9 copy-done.2
  164.6 9.0 %fusion.21 = f32[512,1,256]{0,2,1:T(8,128)S(1)} fusion(f32[2048,256]{1,0:T(8,128)S(1)} %bitcast.71, f32[1,512,2048]{2,1,0:T(8,128)S(1)} %copy-done.2, f32[3,512,2048]{2,1,0:T(8,128)} %param.6), kind=kOutput, calls=%fused_computation.15 | convolution fusion | flops 3222405120 | bytes 11010048 | tf_op jit(solution)/shard_map/nji,niw->jnw/dot_general | solution.py:31
  173.6 1.1 copy.8
  174.7 0.9 all-to-all-done.2
  175.6 0.0 copy-start
  175.6 0.2 broadcast_multiply_fusion
  175.8 2.0 copy-done
  177.8 0.0 copy-start.5
  177.8 9.0 %fusion.27 = f32[512,1,256]{0,2,1:T(8,128)S(1)} fusion(f32[2048,256]{1,0:T(8,128)S(1)} %bitcast.72, f32[1,512,2048]{2,1,0:T(8,128)S(1)} %copy-done, f32[3,512,2048]{2,1,0:T(8,128)} %param.6), kind=kOutput, calls=%fused_computation.17 | convolution fusion | flops 3222405120 | bytes 11010048 | tf_op jit(solution)/shard_map/nji,niw->jnw/dot_general | solution.py:31
  186.8 1.0 copy.9
  187.8 0.0 all-reduce.6.cloned.1.call-update
  187.8 0.0 copy-done.5
  187.9 0.6 dynamic-slice
  189.1 122.3 %all-reduce.6.cloned.1.call-done = (f32[512,1,256]{2,1,0:T(1,128)}, f32[512,1,256]{2,1,0:T(1,128)}, f32[512,1,256]{2,1,0:T(1,128)}) async-done(((f32[512,1,256]{2,1,0:T(1,128)}, f32[512,1,256]{2,1,0:T(1,128)}, f32[512,1,256]{2,1,0:T(1,128)}), (f32[512,1,256]{2,1,0:T(1,128)}, f32[512,1,256]{2,1,0:T(1,128)}, f32[512,1,256]{2,1,0:T(1,128)})) %all-reduce.6.cloned.1.call-update) | async-done | bytes 1572880
  311.4 0.8 dynamic-slice_bitcast_fusion.2
  312.2 0.9 dynamic-slice_bitcast_fusion
  313.1 0.2 pad_maximum_fusion
  313.3 0.7 copy.10
  (2 shorter events, 0.0 us)
Async XLA Ops:
  119.7 7.2 %copy-start.4 = (s32[3,16]{1,0:T(4,128)S(1)}, s32[3,16]{1,0:T(4,128)}, u32[]{:S(2)}) copy-start(s32[3,16]{1,0:T(4,128)} %param.5) | copy-start | bytes 580
  119.7 7.4 %copy-start.3 = (s32[3,4,16]{2,1,0:T(4,128)S(1)}, s32[3,4,16]{2,1,0:T(4,128)}, u32[]{:S(2)}) copy-start(s32[3,4,16]{2,1,0:T(4,128)} %param.7) | copy-start | bytes 2308
  121.2 54.3 %all-to-all-start.2 = ((f32[32,1,64,256]{3,2,1,0:T(8,128)}), f32[32,1,64,256]{3,2,1,0:T(8,128)S(1)}, u32[]{:S(2)}, u32[]{:S(2)}) async-start(f32[32,1,64,256]{3,2,1,0:T(8,128)} %stack.8), calls=%async_computation.2 | async-start | bytes 4194304 | tf_op jit(solution)/shard_map/all_to_all | solution.py:47
  126.8 184.6 %all-reduce.6.cloned.1.call-start = ((), (), s32[]{:S(2)}) async-start(), calls=%async_computation.3 | async-start | bytes 3145728
  148.9 2.8 copy-start.1
  161.8 2.8 copy-start.2
  175.6 2.2 copy-start
  177.8 10.1 %copy-start.5 = (u32[256]{0:T(256)S(1)}, u32[256]{0:T(256)}, u32[]{:S(2)}) copy-start(u32[256]{0:T(256)} %constant.4) | copy-start | bytes 3076
Sparse Core Ops, SparseCore 0:
  188.0 123.3 all-reduce.5
